TPU v7x, 32 devices: a whole 2x2x4 slice. The times are simulated.
32 devices in a mesh: groups: 1, expert: 8 (over y, x, core), tensor: 4 (over z).
Axes of the slice: x: 2, y: 2, z: 4, core: 2. Of those that a mesh axis runs over, the one named last changes fastest.
Arguments:
- attn_partial: bfloat16 [4, 512, 4096], P('tensor', ('groups', 'expert')), may hold values from -6 to 6
- residual: bfloat16 [512, 4096], P(('groups', 'expert', 'tensor')), may hold values from -6 to 6
- norm_gain: float32 [4096], replicated, may hold values from 0.25 to 1.75
- expert_ids: int32 [512, 8], P(('groups', 'expert', 'tensor')), may hold values from 0 to 15, all different within a row; in each aligned block of 16 rows (0 to 15, 16 to 31, ...) at most 16 rows name the same one
- route_weight: int32 [512, 8], P(('groups', 'expert', 'tensor')), may hold values from 256 to 4095
- w_gate: bfloat16 [32, 4096, 384], P(('expert', 'tensor')), may hold values from -0.09375 to 0.09375
- w_up: bfloat16 [32, 4096, 384], P(('expert', 'tensor')), may hold values from -0.09375 to 0.09375
- w_down: bfloat16 [32, 384, 4096], P(('expert', 'tensor')), may hold values from -0.21875 to 0.21875
Outputs:
- layer_out: bfloat16 [512, 4096], P(('groups', 'expert', 'tensor'))
Inputs may be any that keep to these rules, and one draw needn't show every extreme that they name: `expert_ids`: each row names 8 different experts; among the 16 rows of one device no expert is named by more than 16 rows, a bound that some block reaches.
All inputs are finite; a program needn't handle non-finite values.
Results may differ from a plain program's by a relative error of at most 0.015.
Values may be sent and summed in bfloat16 or wider, within the bound.
A program may use at most 64 MiB of HBM per device.

v0:
```python
import jax
import jax.numpy as jnp
from jax import lax
from jax.sharding import PartitionSpec as P

epsilon = 1e-06


def body(attn_partial, residual, norm_gain, expert_ids, route_weight, w_gate, w_up, w_down):
    width = residual.shape[1]
    tok_rows = residual.shape[0]
    top_picks = expert_ids.shape[1]
    n_expert = lax.axis_size("expert")
    n_tensor = lax.axis_size("tensor")
    experts = n_expert * n_tensor // 2
    capacity = max(2, min(tok_rows, 2 * tok_rows * top_picks // experts))
    attn_total = lax.psum_scatter(
        attn_partial[0].astype(jnp.float32).astype(jnp.bfloat16),
        "tensor",
        scatter_dimension=0,
        tiled=True,
    ).astype(jnp.float32)
    stream = residual.astype(jnp.float32) + attn_total
    scale = lax.rsqrt(jnp.mean(stream * stream, axis=-1, keepdims=True) + epsilon)
    normed = (stream * scale * norm_gain).astype(jnp.bfloat16)
    weights = route_weight.astype(jnp.float32) / 2048.0
    picked = expert_ids[None, :, :] == jnp.arange(experts, dtype=jnp.int32)[:, None, None]
    chosen = jnp.any(picked, axis=-1)
    weighting = jnp.sum(jnp.where(picked, weights[None, :, :], jnp.float32(0.0)), axis=-1)
    position = jnp.cumsum(chosen.astype(jnp.int32), axis=1) - 1
    slots = jnp.arange(capacity, dtype=jnp.int32)
    selector = chosen[:, None, :] & (position[:, None, :] == slots[None, :, None])
    gathered = jnp.einsum(
        "ect,td->ecd", selector.astype(jnp.bfloat16), normed, preferred_element_type=jnp.float32
    ).astype(jnp.bfloat16)
    outgoing = jnp.broadcast_to(gathered[:, None], (experts, 2, capacity, width))
    direct_send = outgoing.reshape(n_expert * n_tensor, capacity, width)
    incoming = lax.all_to_all(
        direct_send, ("expert", "tensor"), split_axis=0, concat_axis=0, tiled=True
    )
    flattened = incoming.reshape(-1, width)
    gate_out = jnp.dot(flattened, w_gate[0], preferred_element_type=jnp.float32)
    up_out = jnp.dot(flattened, w_up[0], preferred_element_type=jnp.float32)
    activated = (jax.nn.silu(gate_out) * up_out).astype(jnp.bfloat16)
    half_out = jnp.dot(activated, w_down[0], preferred_element_type=jnp.float32).astype(
        jnp.bfloat16
    )
    returned = lax.all_to_all(
        half_out.reshape(incoming.shape),
        ("expert", "tensor"),
        split_axis=0,
        concat_axis=0,
        tiled=True,
    )
    returned = returned.reshape(experts, 2, capacity, width)
    combined = returned[:, 0].astype(jnp.float32) + returned[:, 1].astype(jnp.float32)
    mixing = selector.astype(jnp.float32) * weighting[:, None, :]
    expert_mix = jnp.einsum("ect,ecd->td", mixing, combined, precision=lax.Precision.HIGHEST)
    return (stream + expert_mix).astype(jnp.bfloat16)


def solution(mesh):
    in_specs = (
        P("tensor", ("groups", "expert"), None),
        P(("groups", "expert", "tensor"), None),
        P(),
        P(("groups", "expert", "tensor"), None),
        P(("groups", "expert", "tensor"), None),
        P(("expert", "tensor"), None, None),
        P(("expert", "tensor"), None, None),
        P(("expert", "tensor"), None, None),
    )
    out_specs = P(("groups", "expert", "tensor"), None)
    return jax.shard_map(body, mesh=mesh, in_specs=in_specs, out_specs=out_specs, check_vma=False)
```

profile of v0, /device:TPU:0, one launch (start us, length us, event | category | flops | bytes accessed | tf_op | source)
XLA Modules:
  0.0 261.1 jit_solution(2754344751475261155)
XLA Ops:
  6.5 0.0 copy-start
  6.5 0.0 reduce-scatter.2.cloned.1.call-start
  6.5 0.7 reduce-scatter.2.cloned.1.call-update
  7.3 0.9 fusion.25
  8.2 0.1 copy.20
  8.3 0.2 reduce_window_sum.11
  8.5 0.1 copy.21
  8.6 0.1 copy.23
  8.7 25.3 %reduce-scatter.2.cloned.1.call-done = bf16[16,4096]{1,0:T(8,128)(2,1)} async-done(((bf16[64,4096]{1,0:T(8,128)(2,1)}), bf16[16,4096]{1,0:T(8,128)(2,1)}) %reduce-scatter.2.cloned.1.call-update) | async-done | bytes 131088 | tf_op jit(solution)/shard_map/reduce_scatter | solution.py:17
  34.0 1.1 multiply_reduce_fusion
  35.2 1.7 convolution_convert_fusion.1
  36.9 0.5 broadcast_in_dim.16
  37.4 0.0 copy-start.6
  37.4 95.2 %all_to_all.10 = bf16[32,16,4096]{2,1,0:T(8,128)(2,1)S(1)} all-to-all(bf16[32,16,4096]{2,1,0:T(8,128)(2,1)S(1)} %bitcast.34), channel_id=1, replica_groups=mesh['groups'=1,'expert'=8,'tensor'=4] {'expert','tensor'}, dimensions={0} | all-to-all | bytes 8388608 | tf_op jit(solution)/shard_map/all_to_all | solution.py:38
  132.6 0.0 copy-start.1
  132.6 2.0 copy-done.1
  134.6 0.0 copy-done.6
  134.6 3.3 %fusion.6 = f32[512,384]{1,0:T(8,128)} fusion(bf16[512,4096]{1,0:T(8,128)(2,1)S(1)} %bitcast.36, bf16[1,4096,384]{2,1,0:T(8,128)(2,1)S(1)} %copy-done.6), kind=kOutput, calls=%fused_computation.10 | convolution fusion | flops 1610612736 | bytes 8126464 | tf_op jit(solution)/shard_map/dot_general | solution.py:42
  137.9 0.0 copy-done
  137.9 9.7 %convolution_convert_fusion = bf16[512,4096]{1,0:T(8,128)(2,1)} fusion(bf16[1,384,4096]{2,1,0:T(8,128)(2,1)S(1)} %copy-done, bf16[512,4096]{1,0:T(8,128)(2,1)} %bitcast.37, bf16[1,4096,384]{2,1,0:T(8,128)(2,1)} %param.14, f32[512,384]{1,0:T(8,128)} %fusion.6), kind=kOutput, calls=%fused_computation | convolution fusion | flops 3224502272 | bytes 15466496 | tf_op jit(solution)/shard_map/dot_general | solution.py:45
  147.6 0.0 copy-start.5
  147.6 0.0 copy-start.4
  147.6 4.8 %all-to-all-start.1 = ((bf16[32,16,4096]{2,1,0:T(8,128)(2,1)}), bf16[32,16,4096]{2,1,0:T(8,128)(2,1)}, u32[]{:S(2)}, u32[]{:S(2)}) async-start(bf16[32,16,4096]{2,1,0:T(8,128)(2,1)} %bitcast.35), calls=%async_computation.2 | async-start | bytes 8388608 | tf_op jit(solution)/shard_map/all_to_all | solution.py:48
  152.3 0.0 copy-done.5
  152.4 0.0 copy-done.4
  152.4 0.1 copy.22
  152.5 91.9 %all-to-all-done.1 = bf16[32,16,4096]{2,1,0:T(8,128)(2,1)} async-done(((bf16[32,16,4096]{2,1,0:T(8,128)(2,1)}), bf16[32,16,4096]{2,1,0:T(8,128)(2,1)}, u32[]{:S(2)}, u32[]{:S(2)}) %all-to-all-start.1) | async-done | bytes 4194336 | tf_op jit(solution)/shard_map/all_to_all | solution.py:48
  244.4 0.0 copy-start.2
  244.4 0.0 copy-start.3
  244.4 3.0 %add_bitcast_fusion = f32[16,16,4096]{2,1,0:T(8,128)S(1)} fusion(bf16[16,2,16,4096]{3,2,1,0:T(8,128)(2,1)} %bitcast.8), kind=kLoop, calls=%fused_computation.6 | loop fusion | flops 3145728 | bytes 8388608 | tf_op jit(solution)/shard_map/add | solution.py:56
  247.4 0.0 copy-done.2
  247.4 0.0 copy-done.3
  247.4 6.9 %fusion.1 = bf16[16,4096]{1,0:T(8,128)(2,1)} fusion(f32[16,16,4096]{2,1,0:T(8,128)S(1)} %add_bitcast_fusion, bf16[16,4096]{1,0:T(8,128)(2,1)S(1)} %copy-done.3, bf16[16,4096]{1,0:T(8,128)(2,1)S(1)} %copy-done.2, f32[16,16]{0,1:T(8,128)S(1)} %copy.22, s32[16,16]{0,1:T(8,128)S(1)} %copy.21, pred[16,16]{0,1:T(8,128)(4,1)S(1)} %copy.20), kind=kOutput, calls=%fused_computation.4 | convolution fusion | flops 201666560 | bytes 4589824 | tf_op jit(solution)/shard_map/ect,ecd->td/dot_general | solution.py:58
  (6 shorter events, 0.1 us)
Async XLA Ops:
  6.5 131.3 %copy-start = (bf16[1,384,4096]{2,1,0:T(8,128)(2,1)S(1)}, bf16[1,384,4096]{2,1,0:T(8,128)(2,1)}, u32[]{:S(2)}) copy-start(bf16[1,384,4096]{2,1,0:T(8,128)(2,1)} %param.15) | copy-start | bytes 9437188
  6.5 27.5 %reduce-scatter.2.cloned.1.call-start = ((), (), s32[]{:S(2)}) async-start(), calls=%async_computation.3 | async-start | bytes 655360 | tf_op jit(solution)/shard_map/reduce_scatter | solution.py:17
  37.4 97.2 %copy-start.6 = (bf16[1,4096,384]{2,1,0:T(8,128)(2,1)S(1)}, bf16[1,4096,384]{2,1,0:T(8,128)(2,1)}, u32[]{:S(2)}) copy-start(bf16[1,4096,384]{2,1,0:T(8,128)(2,1)} %param.13) | copy-start | bytes 9437188
  132.6 2.0 copy-start.1
  147.6 4.8 %copy-start.5 = (s32[16,8]{0,1:T(8,128)S(1)}, s32[16,8]{0,1:T(8,128)}, u32[]{:S(2)}) copy-start(s32[16,8]{0,1:T(8,128)} %param.12) | copy-start | bytes 1540
  147.6 4.8 %copy-start.4 = (s32[16,8]{0,1:T(8,128)S(1)}, s32[16,8]{0,1:T(8,128)}, u32[]{:S(2)}) copy-start(s32[16,8]{0,1:T(8,128)} %param.11) | copy-start | bytes 1540
  147.6 96.8 %all-to-all-start.1 = ((bf16[32,16,4096]{2,1,0:T(8,128)(2,1)}), bf16[32,16,4096]{2,1,0:T(8,128)(2,1)}, u32[]{:S(2)}, u32[]{:S(2)}) async-start(bf16[32,16,4096]{2,1,0:T(8,128)(2,1)} %bitcast.35), calls=%async_computation.2 | async-start | bytes 8388608 | tf_op jit(solution)/shard_map/all_to_all | solution.py:48
  244.4 3.0 %copy-start.2 = (bf16[16,4096]{1,0:T(8,128)(2,1)S(1)}, bf16[16,4096]{1,0:T(8,128)(2,1)}, u32[]{:S(2)}) copy-start(bf16[16,4096]{1,0:T(8,128)(2,1)} %param.9) | copy-start | bytes 393220
  244.4 3.0 %copy-start.3 = (bf16[16,4096]{1,0:T(8,128)(2,1)S(1)}, bf16[16,4096]{1,0:T(8,128)(2,1)}, u32[]{:S(2)}) copy-start(bf16[16,4096]{1,0:T(8,128)(2,1)} %reduce-scatter.2.cloned.1.call-done) | copy-start | bytes 393220
Sparse Core Ops, SparseCore 0:
  9.6 24.3 reduce-scatter.1
where the time goes:
time: 262 us; the launch traced here: 261 us
  waiting for transfers between devices  118 us (45%)
  blocking collectives  95.2 us (36%)
  matrix products  21.6 us (8%)
  between operations  13.5 us (5%)
  other arithmetic  5.3 us (2%)
  starting transfers between devices  4.76 us (2%)
  local copies, waits for them, and re-layouts  2.87 us (1%)
    all_to_all x1, blocking collectives, body(): lax.all_to_all(direct_send, ('expert', 'tensor'), split_axis=0, concat_ax...  95.2 us
    all_to_all x1, waiting for transfers between devices, body(): lax.all_to_all(half_out.reshape(incoming.shape), ('expert', 'tensor'), sp...  91.9 us
    reduce_scatter x1, waiting for transfers between devices, body(): lax.psum_scatter(attn_partial[0].astype(jnp.float32).astype(jnp.bfloat16)...  25.3 us
    dot_general x1, matrix products, body(): jnp.dot(activated, w_down[0], preferred_element_type=jnp.float32)  9.71 us
    dot_general x1, matrix products, body(): jnp.einsum('ect,ecd->td', mixing, combined, precision=lax.Precision.HIGHEST)  6.86 us
  transfers between devices with their start and end apart: 2, of which 2 were waited for; matrix products, arithmetic and copies ran while one was open for 1% of the time, Pallas kernels for 0%

commit v1 on v0

--- a/solution.py
+++ b/solution.py
@@ -1,12 +1,265 @@
+import functools
+
 import jax
 import jax.numpy as jnp
 from jax import lax
+from jax.experimental import pallas as pl
+from jax.experimental.pallas import tpu as pltpu
 from jax.sharding import PartitionSpec as P
 
 epsilon = 1e-06
-
-
-def body(attn_partial, residual, norm_gain, expert_ids, route_weight, w_gate, w_up, w_down):
+MESH = pl.DeviceIdType.MESH
+EXTRA = 128
+
+
+def kernel(
+    attn_ref, res_ref, gain_ref, ids_ref, rw_ref, wg_hbm, wu_hbm, wd_hbm,
+    out_ref,
+    wg, wu, wd, own_attn, attn_in, stream, rows, part, mate_in, s_in, f_in, z_in,
+    w_sem, attn_send, attn_recv, zg_send, zg_recv, pg_send, pg_recv, mg_send, mg_recv,
+    mr_send, mr_recv, sr_send, sr_recv, fr_send, fr_recv, zr_send, zr_recv,
+):
+    width = res_ref.shape[1]
+    tok = res_ref.shape[0]
+    e = lax.axis_index("expert")
+    z = lax.axis_index("tensor")
+    y, x, c = e // 4, (e // 2) % 2, e % 2
+    fx, fy = (x + 1 - c) % 2, (y + c) % 2
+    sx, sy = (x + c) % 2, (y + 1 - c) % 2
+    p_me, p_f, p_s, p_d = 2 * y + x, 2 * fy + fx, 2 * sy + sx, 2 * (1 - y) + (1 - x)
+    mate_core = 1 - c
+
+    def at_z(k):
+        return ((z // 2 + k // 2) % 2) * 2 + (z + k) % 2
+
+    first = {"expert": 2 * p_f + c, "tensor": z}
+    second = {"expert": 2 * p_s + c, "tensor": z}
+    mate = {"expert": 2 * p_me + mate_core, "tensor": z}
+
+    def along(k):
+        return {"expert": e, "tensor": at_z(k)}
+
+    sent = []
+
+    def send(src, dst, send_sem, recv_sem, to):
+        copy = pltpu.make_async_remote_copy(
+            src_ref=src, dst_ref=dst, send_sem=send_sem, recv_sem=recv_sem,
+            device_id=to, device_id_type=MESH,
+        )
+        copy.start()
+        sent.append(copy)
+
+    def arrived(dst, send_sem, recv_sem, frm):
+        pltpu.make_async_remote_copy(
+            src_ref=dst, dst_ref=dst, send_sem=send_sem, recv_sem=recv_sem,
+            device_id=frm, device_id_type=MESH,
+        ).wait_recv()
+
+    loads = [
+        pltpu.make_async_copy(attn_ref.at[z], own_attn, w_sem.at[3]),
+        pltpu.make_async_copy(wg_hbm, wg, w_sem.at[0]),
+        pltpu.make_async_copy(wu_hbm, wu, w_sem.at[1]),
+        pltpu.make_async_copy(wd_hbm, wd, w_sem.at[2]),
+    ]
+    for load in loads:
+        load.start()
+
+    barrier = pltpu.get_barrier_semaphore()
+    for other in (first, second, mate, along(1), along(2), along(3)):
+        pl.semaphore_signal(barrier, inc=1, device_id=other, device_id_type=MESH)
+    pl.semaphore_wait(barrier, 6)
+
+    for k in (1, 2, 3):
+        send(attn_ref.at[at_z(k)], attn_in.at[k - 1], attn_send.at[k - 1], attn_recv.at[k - 1], along(k))
+
+    column = lax.broadcasted_iota(jnp.int32, (tok, EXTRA), 1)
+    whole = jnp.zeros((tok, EXTRA), jnp.int32)
+    for j in range(ids_ref.shape[1]):
+        whole = whole + jnp.where(column % 64 == ids_ref[:, j : j + 1], rw_ref[:, j : j + 1], 0)
+    low = whole & 15
+    pieces = jnp.where(column < 64, whole - low, low)
+    rows[z, c, p_me, :, width:] = pieces.astype(jnp.float32).astype(jnp.bfloat16)
+
+    loads[0].wait()
+    total = res_ref[...].astype(jnp.float32) + own_attn[...].astype(jnp.float32)
+    for k in (1, 2, 3):
+        arrived(attn_in.at[k - 1], attn_send.at[k - 1], attn_recv.at[k - 1], along(k))
+        total = total + attn_in[k - 1].astype(jnp.float32)
+    stream[...] = total
+    scale = lax.rsqrt(jnp.mean(total * total, axis=-1, keepdims=True) + epsilon)
+    rows[z, c, p_me, :, :width] = (stream[...] * scale * gain_ref[...]).astype(jnp.bfloat16)
+
+    def spread(k):
+        q = at_z(k)
+        mine = rows.at[q, c, p_me]
+        send(mine, mine, pg_send.at[k, 0], pg_recv.at[k, 0], first)
+        send(mine, mine, pg_send.at[k, 1], pg_recv.at[k, 1], second)
+        send(mine, mine, mg_send.at[k, 0], mg_recv.at[k, 0], mate)
+
+    def z_step(k):
+        arrived(rows.at[at_z(k), c, p_me], zg_send.at[k - 1], zg_recv.at[k - 1], along(k))
+        spread(k)
+
+    def f_step(k):
+        block = rows.at[at_z(k), c, p_f]
+        arrived(block, pg_send.at[k, 0], pg_recv.at[k, 0], first)
+        send(block, block, pg_send.at[k, 2], pg_recv.at[k, 2], second)
+        send(block, block, mg_send.at[k, 1], mg_recv.at[k, 1], mate)
+
+    def s_step(k):
+        block = rows.at[at_z(k), c, p_s]
+        arrived(block, pg_send.at[k, 1], pg_recv.at[k, 1], second)
+        send(block, block, mg_send.at[k, 2], mg_recv.at[k, 2], mate)
+
+    def d_step(k):
+        block = rows.at[at_z(k), c, p_d]
+        arrived(block, pg_send.at[k, 2], pg_recv.at[k, 2], second)
+        send(block, block, mg_send.at[k, 3], mg_recv.at[k, 3], mate)
+
+    expert = (e * lax.axis_size("tensor") + z) // 2
+
+    def compute(k):
+        q = at_z(k)
+        for j, p in enumerate((p_me, p_s, p_f, p_d)):
+            arrived(rows.at[q, mate_core, p], mg_send.at[k, j], mg_recv.at[k, j], mate)
+        chunk = 8 * tok
+        tail = rows[q, :, :, :, width:].reshape(chunk, EXTRA).astype(jnp.float32)
+        col = lax.broadcasted_iota(jnp.int32, (chunk, EXTRA), 1)
+        weight = jnp.sum(jnp.where(col % 64 == expert, tail, 0.0), axis=-1, keepdims=True) / 2048.0
+        values = rows[q, :, :, :, :width].reshape(chunk, width)
+        gate = jnp.dot(values, wg[...], preferred_element_type=jnp.float32)
+        up = jnp.dot(values, wu[...], preferred_element_type=jnp.float32)
+        act = (gate / (1.0 + jnp.exp(-gate)) * up).astype(jnp.bfloat16)
+        step = min(1024, width)
+        for n in range(0, width, step):
+            half = jnp.dot(act, wd[:, n : n + step], preferred_element_type=jnp.float32)
+            part[k, :, :, :, n : n + step] = (half * weight).astype(jnp.bfloat16).reshape(2, 4, tok, step)
+        send(part.at[k, mate_core], mate_in.at[k], mr_send.at[k], mr_recv.at[k], mate)
+
+    def add(k, p, arriving):
+        part[k, c, p] = (part[k, c, p].astype(jnp.float32) + arriving.astype(jnp.float32)).astype(jnp.bfloat16)
+
+    def back_s(k):
+        arrived(mate_in.at[k], mr_send.at[k], mr_recv.at[k], mate)
+        for j, p in enumerate((p_s, p_d)):
+            add(k, p, mate_in[k, p])
+            send(part.at[k, c, p], s_in.at[k, j], sr_send.at[k, j], sr_recv.at[k, j], second)
+        for p in (p_f, p_me):
+            add(k, p, mate_in[k, p])
+
+    def back_f(k):
+        arrived(s_in.at[k, 1], sr_send.at[k, 1], sr_recv.at[k, 1], second)
+        add(k, p_f, s_in[k, 1])
+        send(part.at[k, c, p_f], f_in.at[k], fr_send.at[k], fr_recv.at[k], first)
+        arrived(s_in.at[k, 0], sr_send.at[k, 0], sr_recv.at[k, 0], second)
+        add(k, p_me, s_in[k, 0])
+
+    def back_z(k):
+        arrived(f_in.at[k], fr_send.at[k], fr_recv.at[k], first)
+        if k == 0:
+            stream[...] = stream[...] + part[0, c, p_me].astype(jnp.float32) + f_in[0].astype(jnp.float32)
+        else:
+            add(k, p_me, f_in[k])
+            send(part.at[k, c, p_me], z_in.at[k - 1], zr_send.at[k - 1], zr_recv.at[k - 1], along(k))
+
+    spread(0)
+    own = rows.at[z, c, p_me]
+    for k in (1, 2, 3):
+        send(own, own, zg_send.at[k - 1], zg_recv.at[k - 1], along(k))
+
+    f_step(0)
+    z_step(1)
+    s_step(0)
+    d_step(0)
+    f_step(1)
+    z_step(2)
+    s_step(1)
+    d_step(1)
+    for load in loads[1:]:
+        load.wait()
+    compute(0)
+    f_step(2)
+    z_step(3)
+    s_step(2)
+    d_step(2)
+    compute(1)
+    back_s(0)
+    f_step(3)
+    s_step(3)
+    d_step(3)
+    compute(2)
+    back_s(1)
+    back_f(0)
+    compute(3)
+    back_s(2)
+    back_f(1)
+    back_z(0)
+    back_s(3)
+    back_f(2)
+    back_z(1)
+    back_f(3)
+    back_z(2)
+    back_z(3)
+
+    total = stream[...]
+    for k in (1, 2, 3):
+        arrived(z_in.at[k - 1], zr_send.at[k - 1], zr_recv.at[k - 1], along(k))
+        total = total + z_in[k - 1].astype(jnp.float32)
+    out_ref[...] = total.astype(out_ref.dtype)
+    for copy in sent:
+        copy.wait_send()
+
+
+def gather_body(attn_partial, residual, norm_gain, expert_ids, route_weight, w_gate, w_up, w_down):
+    tok, width = residual.shape
+    hidden = w_gate.shape[2]
+    bf16 = jnp.bfloat16
+    dma = pltpu.SemaphoreType.DMA
+    vmem = pl.BlockSpec(memory_space=pltpu.VMEM)
+    hbm = pl.BlockSpec(memory_space=pl.ANY)
+    return pl.pallas_call(
+        kernel,
+        out_shape=jax.ShapeDtypeStruct((tok, width), bf16),
+        in_specs=[hbm, vmem, vmem, vmem, vmem, hbm, hbm, hbm],
+        out_specs=vmem,
+        scratch_shapes=[
+            pltpu.VMEM((width, hidden), bf16),
+            pltpu.VMEM((width, hidden), bf16),
+            pltpu.VMEM((hidden, width), bf16),
+            pltpu.VMEM((tok, width), bf16),
+            pltpu.VMEM((3, tok, width), bf16),
+            pltpu.VMEM((tok, width), jnp.float32),
+            pltpu.VMEM((4, 2, 4, tok, width + EXTRA), bf16),
+            pltpu.VMEM((4, 2, 4, tok, width), bf16),
+            pltpu.VMEM((4, 4, tok, width), bf16),
+            pltpu.VMEM((4, 2, tok, width), bf16),
+            pltpu.VMEM((4, tok, width), bf16),
+            pltpu.VMEM((3, tok, width), bf16),
+            dma((4,)),
+            dma((3,)), dma((3,)),
+            dma((3,)), dma((3,)),
+            dma((4, 3)), dma((4, 3)),
+            dma((4, 4)), dma((4, 4)),
+            dma((4,)), dma((4,)),
+            dma((4, 2)), dma((4, 2)),
+            dma((4,)), dma((4,)),
+            dma((3,)), dma((3,)),
+        ],
+        compiler_params=pltpu.CompilerParams(
+            collective_id=0, has_side_effects=True, vmem_limit_bytes=48 * 1024 * 1024
+        ),
+        cost_estimate=pl.CostEstimate(
+            flops=6 * 32 * tok * width * hidden,
+            bytes_accessed=6 * width * hidden,
+            transcendentals=32 * tok * hidden,
+        ),
+    )(
+        attn_partial.reshape(-1, tok, width), residual, norm_gain.reshape(1, width),
+        expert_ids, route_weight, w_gate[0], w_up[0], w_down[0],
+    )
+
+
+def slots_body(attn_partial, residual, norm_gain, expert_ids, route_weight, w_gate, w_up, w_down):
     width = residual.shape[1]
     tok_rows = residual.shape[0]
     top_picks = expert_ids.shape[1]
@@ -71,4 +324,6 @@
         P(("expert", "tensor"), None, None),
     )
     out_specs = P(("groups", "expert", "tensor"), None)
+    dense = (mesh.shape["expert"], mesh.shape["tensor"]) == (8, 4)
+    body = gather_body if dense else slots_body
     return jax.shard_map(body, mesh=mesh, in_specs=in_specs, out_specs=out_specs, check_vma=False)

time: 262 us -> 82.6 us (0.32)
  waiting for transfers between devices: 118 us -> 0 us
  blocking collectives: 95.2 us -> 0 us
  Pallas kernels: 0 us -> 75.5 us
  matrix products: 21.6 us -> 0 us
  between operations: 13.5 us -> 0.01 us
  other arithmetic: 5.3 us -> 0 us
  starting transfers between devices: 4.76 us -> 0 us
  local copies, waits for them, and re-layouts: 2.87 us -> 6.72 us
    all_to_all x1 -> x0, blocking collectives: 95.2 us -> none  [body(): lax.all_to_all(direct_send, ('expert', 'tensor'), split_axis=0, concat_ax...]
    all_to_all x1 -> x0, waiting for transfers between devices: 91.9 us -> none  [body(): lax.all_to_all(half_out.reshape(incoming.shape), ('expert', 'tensor'), sp...]
    pallas_call x0 -> x1, Pallas kernels: none -> 75.5 us  [gather_body(): pl.pallas_call(kernel, out_shape=jax.ShapeDtypeStruct((tok, width), bf16)...]
    reduce_scatter x1 -> x0, waiting for transfers between devices: 25.3 us -> none  [body(): lax.psum_scatter(attn_partial[0].astype(jnp.float32).astype(jnp.bfloat16)...]
    dot_general x4 -> x0, matrix products: 21.6 us -> none  [the longest x1 9.71 us: body(): jnp.dot(activated, w_down[0], preferred_element_type=jnp.float32)]
    all_to_all x1 -> x0, starting transfers between devices: 4.76 us -> none  [body(): lax.all_to_all(half_out.reshape(incoming.shape), ('expert', 'tensor'), sp...]
    unnamed x14 -> x11, local copies, waits for them, and re-layouts: 1.99 us -> 6.72 us
    add x1 -> x0, other arithmetic: 2.99 us -> none  [body(): returned[:, 0].astype(jnp.float32) + returned[:, 1].astype(jnp.float32)]
  transfers between devices with their start and end apart: 2 -> 0, of which waited for: 2 -> 0; matrix products, arithmetic and copies ran while one was open for 1% -> 0% of each run, Pallas kernels for 0% -> 0%
where the time goes in v1:
time: 82.6 us; the launch traced here: 82.3 us
  Pallas kernels  75.5 us (91%)
  local copies, waits for them, and re-layouts  6.72 us (8%)
    pallas_call x1, Pallas kernels, gather_body(): pl.pallas_call(kernel, out_shape=jax.ShapeDtypeStruct((tok, width), bf16)...  75.5 us
    unnamed x11, local copies, waits for them, and re-layouts  6.72 us

profile of v1, /device:TPU:0, one launch (start us, length us, event | category | flops | bytes accessed | tf_op | source)
XLA Modules:
  0.0 82.3 jit_solution(12421805218140671899)
XLA Ops:
  0.0 0.8 copy.9.ids_ref
  0.8 0.8 copy.10.rw_ref
  1.5 0.0 copy-start
  1.5 1.9 %copy-done = bf16[1,4096,384]{2,1,0:T(8,128)(2,1)S(1)} copy-done((bf16[1,4096,384]{2,1,0:T(8,128)(2,1)S(1)}, bf16[1,4096,384]{2,1,0:T(8,128)(2,1)}, u32[]{:S(2)}) %copy-start) | copy-done | bytes 3145752
  3.4 0.0 copy-start.1
  3.4 1.0 %copy-done.1 = bf16[1,64,4096]{2,1,0:T(8,128)(2,1)S(1)} copy-done((bf16[1,64,4096]{2,1,0:T(8,128)(2,1)S(1)}, bf16[1,64,4096]{2,1,0:T(8,128)(2,1)}, u32[]{:S(2)}) %copy-start.1) | copy-done | bytes 524312
  4.4 0.0 copy-start.2
  4.4 0.9 %copy-done.2 = bf16[16,4096]{1,0:T(8,128)(2,1)S(1)} copy-done((bf16[16,4096]{1,0:T(8,128)(2,1)S(1)}, bf16[16,4096]{1,0:T(8,128)(2,1)}, u32[]{:S(2)}) %copy-start.2) | copy-done | bytes 131096
  5.4 0.0 copy-start.3
  5.4 0.7 copy-done.3
  6.1 75.5 %shard_map.82 = bf16[16,4096]{1,0:T(8,128)(2,1)S(1)} custom-call(bf16[4,16,4096]{2,1,0:T(8,128)(2,1)S(1)} %bitcast.6, bf16[16,4096]{1,0:T(8,128)(2,1)S(1)} %copy-done.2, f32[1,4096]{1,0:T(1,128)S(1)} %bitcast.7, s32[16,8]{1,0:T(8,128)S(1)} %copy.9.ids_ref, s32[16,8]{1,0:T(8,128)S(1)} %copy.10.rw_ref, bf16[4096,384]{1,0:T(8,128)(2,1)S(1)} %bitcast.5, ...), custom_call_target="tpu_custom_call" | custom-call | flops 4831838208 | bytes 9437184 | tf_op jit(solution)/shard_map/pallas_call | solution.py:220
  81.6 0.7 copy.12
Async XLA Ops:
  1.5 1.9 %copy-start = (bf16[1,4096,384]{2,1,0:T(8,128)(2,1)S(1)}, bf16[1,4096,384]{2,1,0:T(8,128)(2,1)}, u32[]{:S(2)}) copy-start(bf16[1,4096,384]{2,1,0:T(8,128)(2,1)} %param.13) | copy-start | bytes 9437188
  3.4 1.0 %copy-start.1 = (bf16[1,64,4096]{2,1,0:T(8,128)(2,1)S(1)}, bf16[1,64,4096]{2,1,0:T(8,128)(2,1)}, u32[]{:S(2)}) copy-start(bf16[1,64,4096]{2,1,0:T(8,128)(2,1)} %param.8) | copy-start | bytes 1572868
  4.4 0.9 %copy-start.2 = (bf16[16,4096]{1,0:T(8,128)(2,1)S(1)}, bf16[16,4096]{1,0:T(8,128)(2,1)}, u32[]{:S(2)}) copy-start(bf16[16,4096]{1,0:T(8,128)(2,1)} %res_ref.1) | copy-start | bytes 393220
  5.4 0.7 copy-start.3

commit v2 on v1

--- a/solution.py
+++ b/solution.py
@@ -13,9 +13,9 @@
 
 
 def kernel(
-    attn_ref, res_ref, gain_ref, ids_ref, rw_ref, wg_hbm, wu_hbm, wd_hbm,
+    attn_ref, res_hbm, gain_hbm, ids_hbm, rw_hbm, wg_hbm, wu_hbm, wd_hbm,
     out_ref,
-    wg, wu, wd, own_attn, attn_in, stream, rows, part, mate_in, s_in, f_in, z_in,
+    res_ref, gain_ref, ids_ref, rw_ref, wg, wu, wd, own_attn, attn_in, stream, rows, part, mate_in, s_in, f_in, z_in,
     w_sem, attn_send, attn_recv, zg_send, zg_recv, pg_send, pg_recv, mg_send, mg_recv,
     mr_send, mr_recv, sr_send, sr_recv, fr_send, fr_recv, zr_send, zr_recv,
 ):
@@ -29,15 +29,22 @@
     p_me, p_f, p_s, p_d = 2 * y + x, 2 * fy + fx, 2 * sy + sx, 2 * (1 - y) + (1 - x)
     mate_core = 1 - c
 
+    flip = z // 2
+    inner = z + flip * (3 - 2 * z)
+
     def at_z(k):
-        return ((z // 2 + k // 2) % 2) * 2 + (z + k) % 2
+        near = k + inner * ((k == 0) - (k == 1))
+        return near + flip * (3 - 2 * near)
+
+    def side(k):
+        return (1 - 2 * inner * (k == 1)) * (1 - 2 * flip)
 
     first = {"expert": 2 * p_f + c, "tensor": z}
     second = {"expert": 2 * p_s + c, "tensor": z}
     mate = {"expert": 2 * p_me + mate_core, "tensor": z}
 
-    def along(k):
-        return {"expert": e, "tensor": at_z(k)}
+    def column(other):
+        return {"expert": e, "tensor": other}
 
     sent = []
 
@@ -56,7 +63,11 @@
         ).wait_recv()
 
     loads = [
-        pltpu.make_async_copy(attn_ref.at[z], own_attn, w_sem.at[3]),
+        pltpu.make_async_copy(ids_hbm, ids_ref, w_sem.at[3]),
+        pltpu.make_async_copy(rw_hbm, rw_ref, w_sem.at[4]),
+        pltpu.make_async_copy(attn_ref.at[z], own_attn, w_sem.at[5]),
+        pltpu.make_async_copy(res_hbm, res_ref, w_sem.at[6]),
+        pltpu.make_async_copy(gain_hbm, gain_ref, w_sem.at[7]),
         pltpu.make_async_copy(wg_hbm, wg, w_sem.at[0]),
         pltpu.make_async_copy(wu_hbm, wu, w_sem.at[1]),
         pltpu.make_async_copy(wd_hbm, wd, w_sem.at[2]),
@@ -65,29 +76,44 @@
         load.start()
 
     barrier = pltpu.get_barrier_semaphore()
-    for other in (first, second, mate, along(1), along(2), along(3)):
+    for other in (first, second, mate) + tuple(column((z + k) % 4) for k in (1, 2, 3)):
         pl.semaphore_signal(barrier, inc=1, device_id=other, device_id_type=MESH)
     pl.semaphore_wait(barrier, 6)
 
     for k in (1, 2, 3):
-        send(attn_ref.at[at_z(k)], attn_in.at[k - 1], attn_send.at[k - 1], attn_recv.at[k - 1], along(k))
-
-    column = lax.broadcasted_iota(jnp.int32, (tok, EXTRA), 1)
-    whole = jnp.zeros((tok, EXTRA), jnp.int32)
-    for j in range(ids_ref.shape[1]):
-        whole = whole + jnp.where(column % 64 == ids_ref[:, j : j + 1], rw_ref[:, j : j + 1], 0)
+        other = (z + k) % 4
+        send(attn_ref.at[other], attn_in.at[k - 1], attn_send.at[k - 1], attn_recv.at[k - 1], column(other))
+
+    for load in loads[:2]:
+        load.wait()
+    place = lax.broadcasted_iota(jnp.int32, (EXTRA, tok), 0)
+    whole = jnp.zeros((EXTRA, tok), jnp.int32)
+    for j in range(ids_ref.shape[0]):
+        whole = whole + jnp.where(place % 64 == ids_ref[j : j + 1, :], rw_ref[j : j + 1, :], 0)
     low = whole & 15
-    pieces = jnp.where(column < 64, whole - low, low)
-    rows[z, c, p_me, :, width:] = pieces.astype(jnp.float32).astype(jnp.bfloat16)
-
-    loads[0].wait()
+    pieces = jnp.where(place < 64, whole - low, low).astype(jnp.float32).astype(jnp.bfloat16)
+    line = lax.broadcasted_iota(jnp.int32, (tok, tok), 0)
+    across = lax.broadcasted_iota(jnp.int32, (tok, tok), 1)
+    same = (line == across).astype(jnp.float32).astype(jnp.bfloat16)
+    turned = lax.dot_general(same, pieces, (((1,), (1,)), ((), ())), preferred_element_type=jnp.float32)
+    rows[z, c, p_me, :, width:] = turned.astype(jnp.bfloat16)
+
+    for load in loads[2:5]:
+        load.wait()
     total = res_ref[...].astype(jnp.float32) + own_attn[...].astype(jnp.float32)
     for k in (1, 2, 3):
-        arrived(attn_in.at[k - 1], attn_send.at[k - 1], attn_recv.at[k - 1], along(k))
+        arrived(attn_in.at[k - 1], attn_send.at[k - 1], attn_recv.at[k - 1], column((z + 4 - k) % 4))
         total = total + attn_in[k - 1].astype(jnp.float32)
     stream[...] = total
     scale = lax.rsqrt(jnp.mean(total * total, axis=-1, keepdims=True) + epsilon)
     rows[z, c, p_me, :, :width] = (stream[...] * scale * gain_ref[...]).astype(jnp.bfloat16)
+
+    def hop(slot, q, to):
+        block = rows.at[q, c, p_me]
+        return pltpu.make_async_remote_copy(
+            src_ref=block, dst_ref=block, send_sem=zg_send.at[slot], recv_sem=zg_recv.at[q],
+            device_id=column(to), device_id_type=MESH,
+        )
 
     def spread(k):
         q = at_z(k)
@@ -97,7 +123,14 @@
         send(mine, mine, mg_send.at[k, 0], mg_recv.at[k, 0], mate)
 
     def z_step(k):
-        arrived(rows.at[at_z(k), c, p_me], zg_send.at[k - 1], zg_recv.at[k - 1], along(k))
+        q = at_z(k)
+        block = rows.at[q, c, p_me]
+        arrived(block, zg_send.at[k], zg_recv.at[q], column(z + side(k)))
+
+        @pl.when(inner == 1)
+        def _():
+            hop(k, q, z - side(k)).start()
+
         spread(k)
 
     def f_step(k):
@@ -160,54 +193,72 @@
             stream[...] = stream[...] + part[0, c, p_me].astype(jnp.float32) + f_in[0].astype(jnp.float32)
         else:
             add(k, p_me, f_in[k])
-            send(part.at[k, c, p_me], z_in.at[k - 1], zr_send.at[k - 1], zr_recv.at[k - 1], along(k))
+            send(part.at[k, c, p_me], z_in.at[z], zr_send.at[k - 1], zr_recv.at[z], column(at_z(k)))
+
+    @pl.when(z < 3)
+    def _():
+        hop(0, z, z + 1).start()
+
+    @pl.when(z > 0)
+    def _():
+        hop(4, z, z - 1).start()
 
     spread(0)
-    own = rows.at[z, c, p_me]
-    for k in (1, 2, 3):
-        send(own, own, zg_send.at[k - 1], zg_recv.at[k - 1], along(k))
 
     f_step(0)
     z_step(1)
     s_step(0)
     d_step(0)
+    z_step(2)
     f_step(1)
-    z_step(2)
     s_step(1)
+    z_step(3)
     d_step(1)
-    for load in loads[1:]:
-        load.wait()
+    f_step(2)
+    for load in loads[5:]: load.wait()
     compute(0)
-    f_step(2)
-    z_step(3)
     s_step(2)
     d_step(2)
+    f_step(3)
     compute(1)
-    back_s(0)
-    f_step(3)
     s_step(3)
     d_step(3)
+    back_s(1)
     compute(2)
-    back_s(1)
-    back_f(0)
-    compute(3)
     back_s(2)
     back_f(1)
-    back_z(0)
+    compute(3)
     back_s(3)
     back_f(2)
     back_z(1)
+    back_s(0)
     back_f(3)
     back_z(2)
+    back_f(0)
     back_z(3)
+    back_z(0)
 
     total = stream[...]
     for k in (1, 2, 3):
-        arrived(z_in.at[k - 1], zr_send.at[k - 1], zr_recv.at[k - 1], along(k))
-        total = total + z_in[k - 1].astype(jnp.float32)
+        q = at_z(k)
+        arrived(z_in.at[q], zr_send.at[k - 1], zr_recv.at[q], column(q))
+        total = total + z_in[q].astype(jnp.float32)
     out_ref[...] = total.astype(out_ref.dtype)
     for copy in sent:
         copy.wait_send()
+
+    @pl.when(z < 3)
+    def _():
+        hop(0, z, z + 1).wait_send()
+
+    @pl.when(z > 0)
+    def _():
+        hop(4, z, z - 1).wait_send()
+
+    @pl.when(inner == 1)
+    def _():
+        for k in (1, 2, 3):
+            hop(k, at_z(k), z - side(k)).wait_send()
 
 
 def gather_body(attn_partial, residual, norm_gain, expert_ids, route_weight, w_gate, w_up, w_down):
@@ -220,9 +271,13 @@
     return pl.pallas_call(
         kernel,
         out_shape=jax.ShapeDtypeStruct((tok, width), bf16),
-        in_specs=[hbm, vmem, vmem, vmem, vmem, hbm, hbm, hbm],
+        in_specs=[hbm] * 8,
         out_specs=vmem,
         scratch_shapes=[
+            pltpu.VMEM((tok, width), bf16),
+            pltpu.VMEM((1, width), jnp.float32),
+            pltpu.VMEM(expert_ids.shape[::-1], jnp.int32),
+            pltpu.VMEM(expert_ids.shape[::-1], jnp.int32),
             pltpu.VMEM((width, hidden), bf16),
             pltpu.VMEM((width, hidden), bf16),
             pltpu.VMEM((hidden, width), bf16),
@@ -234,19 +289,19 @@
             pltpu.VMEM((4, 4, tok, width), bf16),
             pltpu.VMEM((4, 2, tok, width), bf16),
             pltpu.VMEM((4, tok, width), bf16),
-            pltpu.VMEM((3, tok, width), bf16),
-            dma((4,)),
+            pltpu.VMEM((4, tok, width), bf16),
+            dma((8,)),
             dma((3,)), dma((3,)),
-            dma((3,)), dma((3,)),
+            dma((5,)), dma((4,)),
             dma((4, 3)), dma((4, 3)),
             dma((4, 4)), dma((4, 4)),
             dma((4,)), dma((4,)),
             dma((4, 2)), dma((4, 2)),
             dma((4,)), dma((4,)),
-            dma((3,)), dma((3,)),
+            dma((3,)), dma((4,)),
         ],
         compiler_params=pltpu.CompilerParams(
-            collective_id=0, has_side_effects=True, vmem_limit_bytes=48 * 1024 * 1024
+            collective_id=0, has_side_effects=True, vmem_limit_bytes=60 * 1024 * 1024
         ),
         cost_estimate=pl.CostEstimate(
             flops=6 * 32 * tok * width * hidden,
@@ -255,7 +310,7 @@
         ),
     )(
         attn_partial.reshape(-1, tok, width), residual, norm_gain.reshape(1, width),
-        expert_ids, route_weight, w_gate[0], w_up[0], w_down[0],
+        expert_ids.T, route_weight.T, w_gate[0], w_up[0], w_down[0],
     )
 
 

time: 82.6 us -> 75.1 us (0.909)
  local copies, waits for them, and re-layouts: 6.72 us -> 1.57 us
  Pallas kernels: 75.5 us -> 73.4 us
    unnamed x11 -> x1, local copies, waits for them, and re-layouts: 6.72 us -> 1.57 us
    pallas_call x1, Pallas kernels: 75.5 us -> 73.4 us  [gather_body(): pl.pallas_call(kernel, out_shape=jax.ShapeDtypeStruct((tok, width), bf16)...]
where the time goes in v2:
time: 75.1 us; the launch traced here: 75 us
  Pallas kernels  73.4 us (98%)
  local copies, waits for them, and re-layouts  1.57 us (2%)
    pallas_call x1, Pallas kernels, gather_body(): pl.pallas_call(kernel, out_shape=jax.ShapeDtypeStruct((tok, width), bf16)...  73.4 us
    unnamed x1, local copies, waits for them, and re-layouts  1.57 us

profile of v2, /device:TPU:0, one launch (start us, length us, event | category | flops | bytes accessed | tf_op | source)
XLA Modules:
  0.0 75.0 jit_solution(18282773793684799891)
XLA Ops:
  0.0 73.4 %shard_map.82 = bf16[16,4096]{1,0:T(8,128)(2,1)} custom-call(bf16[4,16,4096]{2,1,0:T(8,128)(2,1)} %bitcast.10, bf16[16,4096]{1,0:T(8,128)(2,1)} %res_hbm.1, f32[1,4096]{1,0:T(1,128)} %bitcast.11, s32[8,16]{1,0:T(8,128)} %bitcast.12, s32[8,16]{1,0:T(8,128)} %bitcast.13, bf16[4096,384]{1,0:T(8,128)(2,1)} %bitcast.7, bf16[4096,384]{1,0:T(8,128)(2,1)} %bitcast.8, ...), custom_call_target="tpu_custom_call" | custom-call | flops 4831838208 | bytes 9437184 | tf_op jit(solution)/shard_map/pallas_call | solution.py:271
  73.4 1.6 %copy.10 = bf16[16,4096]{1,0:T(8,128)(2,1)} copy(bf16[16,4096]{1,0:T(8,128)(2,1)} %shard_map.82) | data formatting | bytes 262144

commit v3 on v2

--- a/solution.py
+++ b/solution.py
@@ -80,7 +80,7 @@
         pl.semaphore_signal(barrier, inc=1, device_id=other, device_id_type=MESH)
     pl.semaphore_wait(barrier, 6)
 
-    for k in (1, 2, 3):
+    for k in (2, 3, 1):
         other = (z + k) % 4
         send(attn_ref.at[other], attn_in.at[k - 1], attn_send.at[k - 1], attn_recv.at[k - 1], column(other))
 
@@ -208,32 +208,32 @@
     f_step(0)
     z_step(1)
     s_step(0)
+    z_step(2)
     d_step(0)
-    z_step(2)
     f_step(1)
+    z_step(3)
     s_step(1)
-    z_step(3)
     d_step(1)
     f_step(2)
     for load in loads[5:]: load.wait()
     compute(0)
     s_step(2)
+    f_step(3)
     d_step(2)
-    f_step(3)
     compute(1)
+    back_s(1)
     s_step(3)
     d_step(3)
-    back_s(1)
     compute(2)
+    back_f(1)
     back_s(2)
-    back_f(1)
     compute(3)
+    back_z(1)
     back_s(3)
     back_f(2)
-    back_z(1)
     back_s(0)
+    back_z(2)
     back_f(3)
-    back_z(2)
     back_f(0)
     back_z(3)
     back_z(0)

time: 75.1 us -> 73.4 us (0.977)
  Pallas kernels: 73.4 us -> 71.7 us
    pallas_call x1, Pallas kernels: 73.4 us -> 71.7 us  [gather_body(): pl.pallas_call(kernel, out_shape=jax.ShapeDtypeStruct((tok, width), bf16)...]
where the time goes in v3:
time: 73.4 us; the launch traced here: 73.3 us
  Pallas kernels  71.7 us (98%)
  local copies, waits for them, and re-layouts  1.57 us (2%)
    pallas_call x1, Pallas kernels, gather_body(): pl.pallas_call(kernel, out_shape=jax.ShapeDtypeStruct((tok, width), bf16)...  71.7 us
    unnamed x1, local copies, waits for them, and re-layouts  1.57 us

profile of v3, /device:TPU:0, one launch (start us, length us, event | category | flops | bytes accessed | tf_op | source)
XLA Modules:
  0.0 73.3 jit_solution(4264543215879053422)
XLA Ops:
  0.0 71.7 %shard_map.82 = bf16[16,4096]{1,0:T(8,128)(2,1)} custom-call(bf16[4,16,4096]{2,1,0:T(8,128)(2,1)} %bitcast.10, bf16[16,4096]{1,0:T(8,128)(2,1)} %res_hbm.1, f32[1,4096]{1,0:T(1,128)} %bitcast.11, s32[8,16]{1,0:T(8,128)} %bitcast.12, s32[8,16]{1,0:T(8,128)} %bitcast.13, bf16[4096,384]{1,0:T(8,128)(2,1)} %bitcast.7, bf16[4096,384]{1,0:T(8,128)(2,1)} %bitcast.8, ...), custom_call_target="tpu_custom_call" | custom-call | flops 4831838208 | bytes 9437184 | tf_op jit(solution)/shard_map/pallas_call | solution.py:271
  71.7 1.6 %copy.10 = bf16[16,4096]{1,0:T(8,128)(2,1)} copy(bf16[16,4096]{1,0:T(8,128)(2,1)} %shard_map.82) | data formatting | bytes 262144
